TPU v7x, 32 devices: a whole 2x2x4 slice. The times are simulated.
32 devices in a mesh: row: 8 (over y, x, core), col: 4 (over z).
Axes of the slice: x: 2, y: 2, z: 4, core: 2. Of those that a mesh axis runs over, the one named last changes fastest.
Arguments:
- features: bfloat16 [12288, 256], P(('row', 'col')), may hold values from -6 to 6
- weight: bfloat16 [256, 256], replicated, may hold values from -0.375 to 0.375
- out_bias: float32 [256], replicated, may hold values from -3 to 3
- cotangent: bfloat16 [12288, 256], P(('row', 'col')), may hold values from -6 to 6
- adj_tiles: bfloat16 [8, 4, 12, 16, 128, 128], P('row', 'col'), may hold values from -0.125 to 0.125
- tile_cols: int32 [8, 4, 12, 16], P('row', 'col'), may hold values from 0 to 23, as said below
- tile_counts: int32 [8, 4, 12], P('row', 'col'), may hold values from 1 to 16, as said below
Outputs:
- activated: bfloat16 [12288, 256], P(('row', 'col'))
- grad_features: bfloat16 [12288, 256], P(('row', 'col'))
- grad_weight: float32 [256, 256], replicated
- grad_bias: float32 [256], replicated
Inputs may be any that keep to these rules, and one draw needn't show every extreme that they name: `tile_cols`: within a tile row of a block the 16 column numbers are distinct. `tile_counts`: every block has a tile row whose 16 slots are all live.
All inputs are finite; a program needn't handle non-finite values.
Results may differ from a plain program's by a relative error of at most 0.02.
Values may be sent and summed in bfloat16 or wider, within the bound.
A program may use at most 192 MiB of HBM per device.

v0:
```python
import functools

import jax
import jax.numpy as jnp
from jax import lax
from jax.experimental import pallas as pl
from jax.experimental.pallas import tpu as pltpu
from jax.sharding import PartitionSpec as P

MESH = pl.DeviceIdType.MESH
BF = jnp.bfloat16
F32 = jnp.float32


def aligned(index, size):
    return pl.ds(pl.multiple_of(index * size, size), size)


def kernel(
    rows, cols, nd, slots, tile, buffers, scale,
    slot_ref, feat_ref, weight_ref, bias_ref, cot_ref, adj_ref,
    act_ref, gfeat_ref, gweight_ref, gbias_ref,
    dense, panel, part, inbox, total, grads, grad_t, acc, back, sib_in, row_in,
    feat_t, w_out, w_in, w_col, w_all,
    load_sem, ag_send, ag_recv, fw_send, fw_recv, up_send, up_recv, dn_send, dn_recv,
    gu_send, gd_send, g_recv, sb_send, sb_recv, rs_send, rs_recv,
    w1_send, w1_recv, w2_send, w2_recv, w3_send, w3_recv,
    *tiles,
):
    r, z = lax.axis_index("row"), lax.axis_index("col")
    width = feat_ref.shape[1]
    chips = rows // 2
    chip, core = r // 2, r % 2
    sibling = 2 * chip + 1 - core
    per = nd // tile
    group = per * slots
    col_tiles = rows * per
    piece = width // rows

    def remote(src, dst, send, recv, row, col):
        return pltpu.make_async_remote_copy(
            src_ref=src, dst_ref=dst, send_sem=send, recv_sem=recv,
            device_id=(row, col), device_id_type=MESH,
        )

    def load(g):
        return pltpu.make_async_copy(
            adj_ref.at[pl.ds(g * group, group)],
            tiles[g % buffers].at[pl.ds(0, group)],
            load_sem.at[g % buffers],
        )

    for g in range(min(buffers, cols)):
        load(g).start()

    barrier = pltpu.get_barrier_semaphore()
    for o in range(1, rows):
        pl.semaphore_signal(barrier, inc=1, device_id=((r + o) % rows, z), device_id_type=MESH)
    for o in range(1, cols):
        pl.semaphore_signal(barrier, inc=1, device_id=(r, (z + o) % cols), device_id_type=MESH)
    projected = jnp.dot(feat_ref[...], weight_ref[...], preferred_element_type=F32).astype(BF)
    mine = aligned(r, nd)
    panel[mine, :] = projected
    pl.semaphore_wait(barrier, rows + cols - 2)

    def ag(o, to):
        return remote(panel.at[mine], panel.at[mine], ag_send.at[o], ag_recv.at[o], to, z)

    def forward(o):
        src = aligned(2 * ((chip + chips - o) % chips) + core, nd)
        return remote(panel.at[src], panel.at[src], fw_send.at[o], fw_recv.at[o], sibling, z)

    def forward_in(o):
        src = aligned(2 * ((chip + chips - o) % chips) + 1 - core, nd)
        return remote(panel.at[src], panel.at[src], fw_send.at[o], fw_recv.at[o], sibling, z)

    for o in range(1, chips):
        ag(o, 2 * ((chip + o) % chips) + core).start()
    forward(0).start()

    feat_t[...] = feat_ref[...].astype(F32).T.astype(BF)
    for b in range(buffers):
        tiles[b][group] = jnp.zeros((tile, tile), BF)
    for g in range(cols):
        buf = tiles[g % buffers]
        load(g).wait()

        def spread(t, carry, g=g, buf=buf):
            at = aligned(g * per + t, tile)
            for j in range(col_tiles):
                dense[at, pl.ds(j * tile, tile)] = buf[slot_ref[g * per + t, j]]
            return carry

        lax.fori_loop(0, per, spread, 0)
        if g + buffers < cols:
            load(g + buffers).start()

    for o in range(1, chips):
        src = aligned(2 * ((chip + chips - o) % chips) + core, nd)
        remote(panel.at[src], panel.at[src], ag_send.at[o], ag_recv.at[o], r, z).wait_recv()
        forward(o).start()
    for o in range(chips):
        forward_in(o).wait_recv()

    def up_copy(d):
        return remote(part.at[aligned(d, nd)], inbox.at[aligned(d + 1, nd)], up_send.at[d], up_recv.at[d], r, z + 1)

    def up_wait(d):
        remote(part.at[aligned(d, nd)], inbox.at[aligned(d + 1, nd)], up_send.at[d], up_recv.at[d], r, z).wait_recv()

    def down_copy(d):
        return remote(part.at[aligned(d, nd)], inbox.at[aligned(d, nd)], dn_send.at[d], dn_recv.at[d], r, z - 1)

    def down_wait(d):
        remote(part.at[aligned(d, nd)], inbox.at[aligned(d, nd)], dn_send.at[d], dn_recv.at[d], r, z).wait_recv()

    low = (z < cols // 2).astype(jnp.int32)

    def produce(s, carry):
        d = low * (cols - 1 - s) + (1 - low) * s
        at = aligned(d, nd)
        part[at, :] = jnp.dot(dense[at, :], panel[...], preferred_element_type=F32).astype(BF)

        @pl.when((z == 0) & (d > z))
        def _():
            up_copy(d).start()

        @pl.when((z == cols - 1) & (d < z))
        def _():
            down_copy(d).start()

        return carry

    lax.fori_loop(0, cols, produce, 0)

    for s in range(cols):
        d = cols - 1 - s

        @pl.when((d > z) & (z > 0))
        def _(d=d):
            at = pl.ds(d * nd, nd)
            up_wait(d)
            part[at, :] = (part[at, :].astype(F32) + inbox[pl.ds((d + 1) * nd, nd), :].astype(F32)).astype(BF)
            up_copy(d).start()

        @pl.when((s < z) & (z < cols - 1))
        def _(d=s):
            at = pl.ds(d * nd, nd)
            down_wait(d)
            part[at, :] = (part[at, :].astype(F32) + inbox[at, :].astype(F32)).astype(BF)
            down_copy(d).start()

    here = aligned(z, nd)
    total[...] = part[here, :].astype(F32) + bias_ref[...]

    @pl.when(z > 0)
    def _():
        up_wait(z)
        total[...] += inbox[aligned(z + 1, nd), :].astype(F32)

    @pl.when(z < cols - 1)
    def _():
        down_wait(z)
        total[...] += inbox[here, :].astype(F32)

    preact = total[...]
    sig = jax.nn.sigmoid(preact)
    grads[here, :] = (cot_ref[...].astype(F32) * sig * (1.0 + preact * (1.0 - sig))).astype(BF)

    def g_copy(b, send, to):
        return remote(grads.at[aligned(b, nd)], grads.at[aligned(b, nd)], send.at[b], g_recv.at[b], r, to)

    @pl.when(z < cols - 1)
    def _():
        g_copy(z, gu_send, z + 1).start()

    @pl.when(z > 0)
    def _():
        g_copy(z, gd_send, z - 1).start()

    act_ref[...] = (preact * sig).astype(BF)

    span = 2 * nd

    def backward(b, first):
        grad_t[...] = grads[aligned(b, nd), :].astype(F32).T.astype(BF)
        at = aligned(b, nd)

        def step(i, carry):
            lanes = aligned(i, span)
            product = jnp.dot(grad_t[...], dense[at, lanes], preferred_element_type=F32)
            if first:
                acc[:, lanes] = product
            else:
                acc[:, lanes] += product
            return carry

        lax.fori_loop(0, rows // 2, step, 0)

    backward(z, True)
    for o in range(1, cols):

        @pl.when(z - o >= 0)
        def _(o=o):
            g_copy(z - o, gu_send, z).wait_recv()

            @pl.when(z < cols - 1)
            def _():
                g_copy(z - o, gu_send, z + 1).start()

        @pl.when(z + o < cols)
        def _(o=o):
            g_copy(z + o, gd_send, z).wait_recv()

            @pl.when(z > 0)
            def _():
                g_copy(z + o, gd_send, z - 1).start()

        @pl.when(z - o >= 0)
        def _(o=o):
            backward(z - o, False)

        @pl.when(z + o < cols)
        def _(o=o):
            backward(z + o, False)

    def sib_copy(m):
        return remote(back.at[2 * m + 1 - core], sib_in.at[m], sb_send.at[m], sb_recv.at[m], sibling, z)

    def lanes_of(dest):
        return aligned(dest, nd)

    for o in range(chips):
        m = (chip + 1 + o) % chips
        dest = 2 * m + 1 - core
        back[dest] = acc[:, lanes_of(dest)].astype(BF)
        sib_copy(m).start()

    def row_copy(o):
        m = (chip + o) % chips
        return remote(back.at[2 * m + core], row_in.at[o], rs_send.at[o], rs_recv.at[o], 2 * m + core, z)

    for o in range(1, chips):
        m = (chip + o) % chips
        dest = 2 * m + core
        sib_copy(m).wait_recv()
        back[dest] = (acc[:, lanes_of(dest)] + sib_in[m].astype(F32)).astype(BF)
        row_copy(o).start()

    bias_row = jnp.sum(grads[...].astype(F32), axis=0, keepdims=True)
    high = bias_row.astype(BF)
    rest = (bias_row - high.astype(F32)).astype(BF).astype(F32)
    line = lax.broadcasted_iota(jnp.int32, (16, width), 0)
    bias_rows = jnp.where(line == 0, high.astype(F32), jnp.where(line == 1, rest, 0.0)).astype(BF)

    sib_copy(chip).wait_recv()
    summed = acc[:, lanes_of(r)] + sib_in[chip].astype(F32)
    for o in range(1, chips):
        row_copy(o).wait_recv()
        summed = summed + row_in[o].astype(F32)
    gp = summed.T.astype(BF)

    w_part = jnp.dot(feat_t[...], gp, preferred_element_type=F32).astype(BF)
    for i in range(rows):
        w_out[i, pl.ds(0, piece), :] = w_part[i * piece:(i + 1) * piece]
        w_out[i, pl.ds(piece, 16), :] = bias_rows

    def w1(o):
        to = (r + o) % rows
        return remote(w_out.at[to], w_in.at[r], w1_send.at[o], w1_recv.at[o], to, z)

    def w1_wait(o):
        src = (r + rows - o) % rows
        remote(w_out.at[src], w_in.at[src], w1_send.at[o], w1_recv.at[o], src, z).wait_recv()

    for o in range(1, rows):
        w1(o).start()
    w_in[r] = w_out[r]
    gfeat_ref[...] = lax.dot_general(
        gp, weight_ref[...], (((1,), (1,)), ((), ())), preferred_element_type=F32
    ).astype(BF)
    for o in range(1, rows):
        w1_wait(o)
    part_sum = w_in[0].astype(F32)
    for i in range(1, rows):
        part_sum = part_sum + w_in[i].astype(F32)
    w_col[z] = part_sum[:piece].astype(BF)

    def w2(o):
        to = (z + o) % cols
        return remote(w_col.at[z], w_col.at[z], w2_send.at[o], w2_recv.at[o], r, to)

    def w2_wait(o):
        src = (z + cols - o) % cols
        remote(w_col.at[src], w_col.at[src], w2_send.at[o], w2_recv.at[o], r, src).wait_recv()

    for o in range(1, cols):
        w2(o).start()
    gbias_ref[...] = (part_sum[piece:piece + 1] + part_sum[piece + 1:piece + 2]) * scale
    for o in range(1, cols):
        w2_wait(o)
    col_sum = w_col[0].astype(F32)
    for i in range(1, cols):
        col_sum = col_sum + w_col[i].astype(F32)
    w_all[r] = col_sum.astype(BF)

    def w3(o):
        to = (r + o) % rows
        return remote(w_all.at[r], w_all.at[r], w3_send.at[o], w3_recv.at[o], to, z)

    def w3_wait(o):
        src = (r + rows - o) % rows
        remote(w_all.at[src], w_all.at[src], w3_send.at[o], w3_recv.at[o], src, z).wait_recv()

    for o in range(1, rows):
        w3(o).start()

    for o in range(1, chips):
        ag(o, 2 * ((chip + o) % chips) + core).wait_send()
        row_copy(o).wait_send()
    for o in range(chips):
        forward(o).wait_send()
        sib_copy((chip + 1 + o) % chips).wait_send()
    for d in range(cols):

        @pl.when(d > z)
        def _(d=d):
            up_copy(d).wait_send()

        @pl.when(d < z)
        def _(d=d):
            down_copy(d).wait_send()

        @pl.when((d <= z) & (z < cols - 1))
        def _(d=d):
            g_copy(d, gu_send, z + 1).wait_send()

        @pl.when((d >= z) & (z > 0))
        def _(d=d):
            g_copy(d, gd_send, z - 1).wait_send()

    for o in range(1, cols):
        w2(o).wait_send()
    for o in range(1, rows):
        w1(o).wait_send()
        w3_wait(o)
    for i in range(rows):
        gweight_ref[pl.ds(i * piece, piece), :] = w_all[i].astype(F32) * scale
    for o in range(1, rows):
        w3(o).wait_send()


def shards(features, weight, out_bias, cotangent, adj_tiles, tile_cols, tile_counts):
    nd, width = features.shape
    tile = adj_tiles.shape[-1]
    slots = adj_tiles.shape[3]
    tile_rows = adj_tiles.shape[2]
    rows, cols = lax.axis_size("row"), lax.axis_size("col")
    per = nd // tile
    col_tiles = rows * per
    chips = rows // 2
    blocks = adj_tiles.reshape(tile_rows * slots, tile, tile)
    columns = tile_cols.reshape(tile_rows, slots)
    counts = tile_counts.reshape(tile_rows)
    k = lax.broadcasted_iota(jnp.int32, (tile_rows, slots, col_tiles), 1)
    j = lax.broadcasted_iota(jnp.int32, (tile_rows, slots, col_tiles), 2)
    t = lax.broadcasted_iota(jnp.int32, (tile_rows, slots, col_tiles), 0)
    found = (columns[:, :, None] == j) & (k < counts[:, None, None])
    slot = jnp.min(jnp.where(found, (t % per) * slots + k, per * slots), axis=1)
    big = tile_rows * col_tiles * tile * tile * 2 > 16 * 2**20
    buffers = 2 if big else min(4, cols)
    piece = width // rows
    dma = lambda n: pltpu.SemaphoreType.DMA((n,))
    vmem = pl.BlockSpec(memory_space=pltpu.VMEM)
    scale = (nd * rows * cols) ** (-0.5)
    act, gfeat, gweight, gbias = pl.pallas_call(
        functools.partial(kernel, rows, cols, nd, slots, tile, buffers, scale),
        out_shape=(
            jax.ShapeDtypeStruct((nd, width), BF),
            jax.ShapeDtypeStruct((nd, width), BF),
            jax.ShapeDtypeStruct((width, width), F32),
            jax.ShapeDtypeStruct((1, width), F32),
        ),
        in_specs=[pl.BlockSpec(memory_space=pltpu.SMEM)] + [vmem] * 4 + [pl.BlockSpec(memory_space=pl.ANY)],
        out_specs=(vmem,) * 4,
        scratch_shapes=[
            pltpu.VMEM((tile_rows * tile, col_tiles * tile), BF),
            pltpu.VMEM((rows * nd, width), BF),
            pltpu.VMEM((cols * nd, width), BF),
            pltpu.VMEM(((cols + 1) * nd, width), BF),
            pltpu.VMEM((nd, width), F32),
            pltpu.VMEM((cols * nd, width), BF),
            pltpu.VMEM((width, nd), BF),
            pltpu.VMEM((width, rows * nd), F32),
            pltpu.VMEM((rows, width, nd), BF),
            pltpu.VMEM((chips, width, nd), BF),
            pltpu.VMEM((chips, width, nd), BF),
            pltpu.VMEM((width, nd), BF),
            pltpu.VMEM((rows, piece + 16, width), BF),
            pltpu.VMEM((rows, piece + 16, width), BF),
            pltpu.VMEM((cols, piece, width), BF),
            pltpu.VMEM((rows, piece, width), BF),
            dma(buffers),
            dma(chips), dma(chips), dma(chips), dma(chips),
            dma(cols), dma(cols), dma(cols), dma(cols),
            dma(cols), dma(cols), dma(cols),
            dma(chips), dma(chips), dma(chips), dma(chips),
            dma(rows), dma(rows), dma(cols), dma(cols), dma(rows), dma(rows),
        ] + [pltpu.VMEM((per * slots + 1, tile, tile), BF)] * buffers,
        compiler_params=pltpu.CompilerParams(
            collective_id=0, has_side_effects=True, vmem_limit_bytes=(63 if big else 48) * 2**20
        ),
    )(slot, features, weight, out_bias.reshape(1, width), cotangent, blocks)
    return act, gfeat, gweight, gbias.reshape(width)


def solution(mesh):
    in_specs = (
        P(("row", "col"), None),
        P(),
        P(),
        P(("row", "col"), None),
        P("row", "col", None, None, None, None),
        P("row", "col", None, None),
        P("row", "col", None),
    )
    out_specs = (P(("row", "col"), None), P(("row", "col"), None), P(), P())
    return jax.shard_map(shards, mesh=mesh, in_specs=in_specs, out_specs=out_specs, check_vma=False)
```

profile of v0, /device:TPU:0, one launch (start us, length us, event | category | flops | bytes accessed | tf_op | source)
XLA Modules:
  0.0 92.8 jit_solution(2156210564936089103)
XLA Ops:
  0.7 0.7 copy.13
  1.4 0.8 select_reduce_fusion.slot_ref
  2.2 0.0 copy-start
  2.2 0.9 copy-done
  3.1 0.0 copy-start.1
  3.1 0.9 copy-done.1
  4.0 0.0 copy-start.2
  4.0 0.9 copy-done.2
  4.9 0.0 copy-start.3
  4.9 0.7 copy-done.3
  5.6 84.5 %shard_map.102 = (bf16[384,256]{1,0:T(8,128)(2,1)S(1)}, bf16[384,256]{1,0:T(8,128)(2,1)S(1)}, f32[256,256]{1,0:T(8,128)S(1)}, f32[1,256]{1,0:T(1,128)S(1)}) custom-call(s32[12,24]{1,0:T(8,128)S(1)} %select_reduce_fusion.slot_ref, bf16[384,256]{1,0:T(8,128)(2,1)S(1)} %copy-done, bf16[256,256]{1,0:T(8,128)(2,1)S(1)} %copy-done.2, f32[1,256]{1,0:T(1,128)S(1)} %bitcast.7, ...), custom_call_target="tpu_custom_call" | custom-call | tf_op jit(solution)/shard_map/pallas_call | solution.py:376
  90.1 0.7 copy.18
  90.8 0.7 copy.19
  91.5 0.7 copy.20
  92.2 0.6 copy.21
  (2 shorter events, 0.0 us)
Async XLA Ops:
  2.2 0.9 %copy-start = (bf16[384,256]{1,0:T(8,128)(2,1)S(1)}, bf16[384,256]{1,0:T(8,128)(2,1)}, u32[]{:S(2)}) copy-start(bf16[384,256]{1,0:T(8,128)(2,1)} %feat_ref.1) | copy-start | bytes 589828
  3.1 0.9 copy-start.1
  4.0 0.9 copy-start.2
  4.9 0.7 copy-start.3
where the time goes:
time: 93 us; the launch traced here: 92.8 us
  Pallas kernels  84.5 us (91%)
  local copies, waits for them, and re-layouts  6.75 us (7%)
    pallas_call x1, Pallas kernels, shards(): pl.pallas_call(functools.partial(kernel, rows, cols, nd, slots, tile, buf...  84.5 us
    unnamed x13, local copies, waits for them, and re-layouts  6.75 us

commit v1 on v0

--- a/solution.py
+++ b/solution.py
@@ -123,10 +123,18 @@
 
         @pl.when((z == 0) & (d > z))
         def _():
+            @pl.when(s > 0)
+            def _():
+                up_copy(d + 1).wait_send()
+
             up_copy(d).start()
 
         @pl.when((z == cols - 1) & (d < z))
         def _():
+            @pl.when(s > 0)
+            def _():
+                down_copy(d - 1).wait_send()
+
             down_copy(d).start()
 
         return carry
@@ -323,11 +331,11 @@
         sib_copy((chip + 1 + o) % chips).wait_send()
     for d in range(cols):
 
-        @pl.when(d > z)
+        @pl.when((d > z) & ((z > 0) | (d == z + 1)))
         def _(d=d):
             up_copy(d).wait_send()
 
-        @pl.when(d < z)
+        @pl.when((d < z) & ((z < cols - 1) | (d == z - 1)))
         def _(d=d):
             down_copy(d).wait_send()
 

time: 93 us -> 89.6 us (0.963)
  Pallas kernels: 84.5 us -> 81.1 us
    pallas_call x1, Pallas kernels: 84.5 us -> 81.1 us  [shards(): pl.pallas_call(functools.partial(kernel, rows, cols, nd, slots, tile, buf...]
where the time goes in v1:
time: 89.6 us; the launch traced here: 89.3 us
  Pallas kernels  81.1 us (91%)
  local copies, waits for them, and re-layouts  6.75 us (8%)
    pallas_call x1, Pallas kernels, shards(): pl.pallas_call(functools.partial(kernel, rows, cols, nd, slots, tile, buf...  81.1 us
    unnamed x13, local copies, waits for them, and re-layouts  6.75 us

profile of v1, /device:TPU:0, one launch (start us, length us, event | category | flops | bytes accessed | tf_op | source)
XLA Modules:
  0.0 89.3 jit_solution(12076417147681245010)
XLA Ops:
  0.7 0.7 copy.13
  1.4 0.8 select_reduce_fusion.slot_ref
  2.2 0.0 copy-start
  2.2 0.9 %copy-done = bf16[384,256]{1,0:T(8,128)(2,1)S(1)} copy-done((bf16[384,256]{1,0:T(8,128)(2,1)S(1)}, bf16[384,256]{1,0:T(8,128)(2,1)}, u32[]{:S(2)}) %copy-start) | copy-done | bytes 196632
  3.1 0.0 copy-start.1
  3.1 0.9 %copy-done.1 = bf16[384,256]{1,0:T(8,128)(2,1)S(1)} copy-done((bf16[384,256]{1,0:T(8,128)(2,1)S(1)}, bf16[384,256]{1,0:T(8,128)(2,1)}, u32[]{:S(2)}) %copy-start.1) | copy-done | bytes 196632
  4.0 0.0 copy-start.2
  4.0 0.9 %copy-done.2 = bf16[256,256]{1,0:T(8,128)(2,1)S(1)} copy-done((bf16[256,256]{1,0:T(8,128)(2,1)S(1)}, bf16[256,256]{1,0:T(8,128)(2,1)}, u32[]{:S(2)}) %copy-start.2) | copy-done | bytes 131096
  4.9 0.0 copy-start.3
  4.9 0.7 copy-done.3
  5.6 81.1 %shard_map.102 = (bf16[384,256]{1,0:T(8,128)(2,1)S(1)}, bf16[384,256]{1,0:T(8,128)(2,1)S(1)}, f32[256,256]{1,0:T(8,128)S(1)}, f32[1,256]{1,0:T(1,128)S(1)}) custom-call(s32[12,24]{1,0:T(8,128)S(1)} %select_reduce_fusion.slot_ref, bf16[384,256]{1,0:T(8,128)(2,1)S(1)} %copy-done, bf16[256,256]{1,0:T(8,128)(2,1)S(1)} %copy-done.2, f32[1,256]{1,0:T(1,128)S(1)} %bitcast.7, ...), custom_call_target="tpu_custom_call" | custom-call | tf_op jit(solution)/shard_map/pallas_call | solution.py:384
  86.7 0.7 copy.18
  87.4 0.7 copy.19
  88.1 0.7 copy.20
  88.8 0.6 copy.21
  (2 shorter events, 0.0 us)
Async XLA Ops:
  2.2 0.9 %copy-start = (bf16[384,256]{1,0:T(8,128)(2,1)S(1)}, bf16[384,256]{1,0:T(8,128)(2,1)}, u32[]{:S(2)}) copy-start(bf16[384,256]{1,0:T(8,128)(2,1)} %feat_ref.1) | copy-start | bytes 589828
  3.1 0.9 %copy-start.1 = (bf16[384,256]{1,0:T(8,128)(2,1)S(1)}, bf16[384,256]{1,0:T(8,128)(2,1)}, u32[]{:S(2)}) copy-start(bf16[384,256]{1,0:T(8,128)(2,1)} %cot_ref.1) | copy-start | bytes 589828
  4.0 0.9 %copy-start.2 = (bf16[256,256]{1,0:T(8,128)(2,1)S(1)}, bf16[256,256]{1,0:T(8,128)(2,1)}, u32[]{:S(2)}) copy-start(bf16[256,256]{1,0:T(8,128)(2,1)} %weight_ref.1) | copy-start | bytes 393220
  4.9 0.7 copy-start.3

commit v2 on v1

--- a/solution.py
+++ b/solution.py
@@ -102,17 +102,19 @@
     for o in range(chips):
         forward_in(o).wait_recv()
 
+    half = nd // 2
+
     def up_copy(d):
-        return remote(part.at[aligned(d, nd)], inbox.at[aligned(d + 1, nd)], up_send.at[d], up_recv.at[d], r, z + 1)
+        return remote(part.at[aligned(d, half)], inbox.at[aligned(d + 2, half)], up_send.at[d], up_recv.at[d], r, z + 1)
 
     def up_wait(d):
-        remote(part.at[aligned(d, nd)], inbox.at[aligned(d + 1, nd)], up_send.at[d], up_recv.at[d], r, z).wait_recv()
+        remote(part.at[aligned(d, half)], inbox.at[aligned(d + 2, half)], up_send.at[d], up_recv.at[d], r, z).wait_recv()
 
     def down_copy(d):
-        return remote(part.at[aligned(d, nd)], inbox.at[aligned(d, nd)], dn_send.at[d], dn_recv.at[d], r, z - 1)
+        return remote(part.at[aligned(d, half)], inbox.at[aligned(d, half)], dn_send.at[d], dn_recv.at[d], r, z - 1)
 
     def down_wait(d):
-        remote(part.at[aligned(d, nd)], inbox.at[aligned(d, nd)], dn_send.at[d], dn_recv.at[d], r, z).wait_recv()
+        remote(part.at[aligned(d, half)], inbox.at[aligned(d, half)], dn_send.at[d], dn_recv.at[d], r, z).wait_recv()
 
     low = (z < cols // 2).astype(jnp.int32)
 
@@ -125,17 +127,21 @@
         def _():
             @pl.when(s > 0)
             def _():
-                up_copy(d + 1).wait_send()
-
-            up_copy(d).start()
+                up_copy(2 * d + 3).wait_send()
+
+            up_copy(2 * d).start()
+            up_copy(2 * d).wait_send()
+            up_copy(2 * d + 1).start()
 
         @pl.when((z == cols - 1) & (d < z))
         def _():
             @pl.when(s > 0)
             def _():
-                down_copy(d - 1).wait_send()
-
-            down_copy(d).start()
+                down_copy(2 * d - 1).wait_send()
+
+            down_copy(2 * d).start()
+            down_copy(2 * d).wait_send()
+            down_copy(2 * d + 1).start()
 
         return carry
 
@@ -146,29 +152,33 @@
 
         @pl.when((d > z) & (z > 0))
         def _(d=d):
-            at = pl.ds(d * nd, nd)
-            up_wait(d)
-            part[at, :] = (part[at, :].astype(F32) + inbox[pl.ds((d + 1) * nd, nd), :].astype(F32)).astype(BF)
-            up_copy(d).start()
+            for u in (2 * d, 2 * d + 1):
+                at = pl.ds(u * half, half)
+                up_wait(u)
+                part[at, :] = (part[at, :].astype(F32) + inbox[pl.ds((u + 2) * half, half), :].astype(F32)).astype(BF)
+                up_copy(u).start()
 
         @pl.when((s < z) & (z < cols - 1))
         def _(d=s):
-            at = pl.ds(d * nd, nd)
-            down_wait(d)
-            part[at, :] = (part[at, :].astype(F32) + inbox[at, :].astype(F32)).astype(BF)
-            down_copy(d).start()
+            for u in (2 * d, 2 * d + 1):
+                at = pl.ds(u * half, half)
+                down_wait(u)
+                part[at, :] = (part[at, :].astype(F32) + inbox[at, :].astype(F32)).astype(BF)
+                down_copy(u).start()
 
     here = aligned(z, nd)
     total[...] = part[here, :].astype(F32) + bias_ref[...]
 
     @pl.when(z > 0)
     def _():
-        up_wait(z)
+        up_wait(2 * z)
+        up_wait(2 * z + 1)
         total[...] += inbox[aligned(z + 1, nd), :].astype(F32)
 
     @pl.when(z < cols - 1)
     def _():
-        down_wait(z)
+        down_wait(2 * z)
+        down_wait(2 * z + 1)
         total[...] += inbox[here, :].astype(F32)
 
     preact = total[...]
@@ -331,13 +341,21 @@
         sib_copy((chip + 1 + o) % chips).wait_send()
     for d in range(cols):
 
+        @pl.when((d > z) & (z > 0))
+        def _(d=d):
+            up_copy(2 * d).wait_send()
+
         @pl.when((d > z) & ((z > 0) | (d == z + 1)))
         def _(d=d):
-            up_copy(d).wait_send()
+            up_copy(2 * d + 1).wait_send()
+
+        @pl.when((d < z) & (z < cols - 1))
+        def _(d=d):
+            down_copy(2 * d).wait_send()
 
         @pl.when((d < z) & ((z < cols - 1) | (d == z - 1)))
         def _(d=d):
-            down_copy(d).wait_send()
+            down_copy(2 * d + 1).wait_send()
 
         @pl.when((d <= z) & (z < cols - 1))
         def _(d=d):
@@ -410,7 +428,7 @@
             pltpu.VMEM((rows, piece, width), BF),
             dma(buffers),
             dma(chips), dma(chips), dma(chips), dma(chips),
-            dma(cols), dma(cols), dma(cols), dma(cols),
+            dma(2 * cols), dma(2 * cols), dma(2 * cols), dma(2 * cols),
             dma(cols), dma(cols), dma(cols),
             dma(chips), dma(chips), dma(chips), dma(chips),
             dma(rows), dma(rows), dma(cols), dma(cols), dma(rows), dma(rows),

time: 89.6 us -> 88.1 us (0.983)
  Pallas kernels: 81.1 us -> 79.6 us
    pallas_call x1, Pallas kernels: 81.1 us -> 79.6 us  [shards(): pl.pallas_call(functools.partial(kernel, rows, cols, nd, slots, tile, buf...]
where the time goes in v2:
time: 88.1 us; the launch traced here: 87.9 us
  Pallas kernels  79.6 us (90%)
  local copies, waits for them, and re-layouts  6.75 us (8%)
    pallas_call x1, Pallas kernels, shards(): pl.pallas_call(functools.partial(kernel, rows, cols, nd, slots, tile, buf...  79.6 us
    unnamed x13, local copies, waits for them, and re-layouts  6.75 us

profile of v2, /device:TPU:0, one launch (start us, length us, event | category | flops | bytes accessed | tf_op | source)
XLA Modules:
  0.0 87.9 jit_solution(5228847704795671571)
XLA Ops:
  0.7 0.7 copy.13
  1.4 0.8 select_reduce_fusion.slot_ref
  2.2 0.0 copy-start
  2.2 0.9 %copy-done = bf16[384,256]{1,0:T(8,128)(2,1)S(1)} copy-done((bf16[384,256]{1,0:T(8,128)(2,1)S(1)}, bf16[384,256]{1,0:T(8,128)(2,1)}, u32[]{:S(2)}) %copy-start) | copy-done | bytes 196632
  3.1 0.0 copy-start.1
  3.1 0.9 %copy-done.1 = bf16[384,256]{1,0:T(8,128)(2,1)S(1)} copy-done((bf16[384,256]{1,0:T(8,128)(2,1)S(1)}, bf16[384,256]{1,0:T(8,128)(2,1)}, u32[]{:S(2)}) %copy-start.1) | copy-done | bytes 196632
  4.0 0.0 copy-start.2
  4.0 0.9 %copy-done.2 = bf16[256,256]{1,0:T(8,128)(2,1)S(1)} copy-done((bf16[256,256]{1,0:T(8,128)(2,1)S(1)}, bf16[256,256]{1,0:T(8,128)(2,1)}, u32[]{:S(2)}) %copy-start.2) | copy-done | bytes 131096
  4.9 0.0 copy-start.3
  4.9 0.7 copy-done.3
  5.6 79.6 %shard_map.102 = (bf16[384,256]{1,0:T(8,128)(2,1)S(1)}, bf16[384,256]{1,0:T(8,128)(2,1)S(1)}, f32[256,256]{1,0:T(8,128)S(1)}, f32[1,256]{1,0:T(1,128)S(1)}) custom-call(s32[12,24]{1,0:T(8,128)S(1)} %select_reduce_fusion.slot_ref, bf16[384,256]{1,0:T(8,128)(2,1)S(1)} %copy-done, bf16[256,256]{1,0:T(8,128)(2,1)S(1)} %copy-done.2, f32[1,256]{1,0:T(1,128)S(1)} %bitcast.7, ...), custom_call_target="tpu_custom_call" | custom-call | tf_op jit(solution)/shard_map/pallas_call | solution.py:402
  85.3 0.7 copy.18
  85.9 0.7 copy.19
  86.6 0.7 copy.20
  87.3 0.6 copy.21
  (2 shorter events, 0.0 us)
Async XLA Ops:
  2.2 0.9 %copy-start = (bf16[384,256]{1,0:T(8,128)(2,1)S(1)}, bf16[384,256]{1,0:T(8,128)(2,1)}, u32[]{:S(2)}) copy-start(bf16[384,256]{1,0:T(8,128)(2,1)} %feat_ref.1) | copy-start | bytes 589828
  3.1 0.9 %copy-start.1 = (bf16[384,256]{1,0:T(8,128)(2,1)S(1)}, bf16[384,256]{1,0:T(8,128)(2,1)}, u32[]{:S(2)}) copy-start(bf16[384,256]{1,0:T(8,128)(2,1)} %cot_ref.1) | copy-start | bytes 589828
  4.0 0.9 %copy-start.2 = (bf16[256,256]{1,0:T(8,128)(2,1)S(1)}, bf16[256,256]{1,0:T(8,128)(2,1)}, u32[]{:S(2)}) copy-start(bf16[256,256]{1,0:T(8,128)(2,1)} %weight_ref.1) | copy-start | bytes 393220
  4.9 0.7 copy-start.3
